TPU v7x, 512 devices: a whole 4x8x8 slice. The times are simulated.
512 devices in a mesh: section: 8 (over y_hi, core), dp: 64 (over x, z, y_lo).
Axes of the slice: x: 4, y: 8 (y_hi: 4, y_lo: 2; y = y_hi * 2 + y_lo), z: 8, core: 2. Of those that a mesh axis runs over, the one named last changes fastest.
Arguments:
- inputs: bfloat16 [2, 4096, 4096], P(None, 'dp'), may hold values from -6 to 6
- cotangent: bfloat16 [2, 4096, 4096], P(None, 'dp'), may hold values from -6 to 6
- doc_lengths: int32 [2, 64, 2], P(None, 'dp'), may hold values from 1 to 48, 64 in all within a row
- norm_gain: bfloat16 [8, 4096], P('section'), may hold values from 0.25 to 1.75
- w_qkv: bfloat16 [8, 4096, 192], P('section', 'dp'), may hold values from -0.09375 to 0.09375
- w_out: bfloat16 [8, 64, 4096], P('section', None, 'dp'), may hold values from -0.75 to 0.75
Outputs:
- grad_qkv: float32 [8, 4096, 192], P('section', 'dp')
- grad_out: float32 [8, 64, 4096], P('section', None, 'dp')
Inputs may be any that keep to these rules, and one draw needn't show every extreme that they name: `doc_lengths`: each row's 2 lengths add up to 64.
All inputs are finite; a program needn't handle non-finite values.
Results may differ from a plain program's by a relative error of at most 0.025.
Values may be sent and summed in bfloat16 or wider, within the bound.
A program may use at most 64 MiB of HBM per device.

v0:
```python
import jax
import jax.numpy as jnp
from jax import lax
from jax.sharding import PartitionSpec as P


def passed_along(block, axis, distance):
    devices = range(lax.axis_size(axis))
    route = [(i - distance, i) for i in devices if i - distance in devices]
    return lax.ppermute(block, axis, route)


def segments_of(lengths, count):
    ends = jnp.cumsum(lengths)
    position = jnp.arange(count, dtype=jnp.int32)
    return jnp.sum((position[:, None] >= ends[None, :]).astype(jnp.int32), axis=1)


def layer(x, gain, w_qkv, w_out, seg):
    head = w_out.shape[0]
    x_wide = x.astype(jnp.float32)
    scale = lax.rsqrt(jnp.mean(x_wide * x_wide, axis=-1, keepdims=True) + 1e-05)
    normed = (x_wide * scale * gain.astype(jnp.float32)).astype(jnp.bfloat16)
    qkv = jnp.dot(normed, w_qkv, preferred_element_type=jnp.float32).astype(jnp.bfloat16)
    query = qkv[:, :head]
    keys = qkv[:, head : 2 * head]
    values = qkv[:, 2 * head :]
    scores = jnp.dot(query, keys.T, preferred_element_type=jnp.float32) * head ** (-0.5)
    rows = jnp.arange(x.shape[0], dtype=jnp.int32)
    allowed = (seg[:, None] == seg[None, :]) & (rows[:, None] >= rows[None, :])
    scores = jnp.where(allowed, scores, -1e30)
    probs = jax.nn.softmax(scores, axis=-1).astype(jnp.bfloat16)
    attended = jnp.dot(probs, values, preferred_element_type=jnp.float32).astype(jnp.bfloat16)
    return (x_wide + jnp.dot(attended, w_out, preferred_element_type=jnp.float32)).astype(
        jnp.bfloat16
    )


def body(inputs, cotangent, doc_lengths, norm_gain, w_qkv, w_out):
    sections = lax.axis_size("section")
    section = lax.axis_index("section")
    micro = inputs.shape[0]
    count = inputs.shape[1]
    segs = jax.vmap(lambda lens: segments_of(lens, count))(doc_lengths[:, 0, :])
    gain = norm_gain[0]
    full_qkv, full_out = (
        lax.all_gather(w_qkv[0], "dp", axis=0, tiled=True),
        lax.all_gather(w_out[0], "dp", axis=1, tiled=True),
    )
    total_steps = micro + sections - 1
    empty = jnp.zeros(inputs.shape[1:], inputs.dtype)

    def forward_at(step, incoming, saved):
        index = step - section
        live = (index >= 0) & (index < micro)
        slot = jnp.clip(index, 0, micro - 1)
        first = lax.dynamic_index_in_dim(inputs, slot, 0, keepdims=False)
        x = jnp.where(section == 0, first, incoming)
        seg = lax.dynamic_index_in_dim(segs, slot, 0, keepdims=False)
        out = layer(x, gain, full_qkv, full_out, seg)
        old = lax.dynamic_index_in_dim(saved, slot, 0, keepdims=False)
        saved = lax.dynamic_update_index_in_dim(saved, jnp.where(live, x, old), slot, 0)
        return (out, saved)

    def forward_step(carry, step):
        incoming, saved = carry
        out, saved = forward_at(step, incoming, saved)
        incoming = passed_along(out, "section", 1)
        return ((incoming, saved), None)

    start_saved = jnp.zeros(inputs.shape, inputs.dtype)
    (incoming, saved), _ = lax.scan(
        forward_step, (empty, start_saved), jnp.arange(total_steps - 1, dtype=jnp.int32)
    )
    _, saved = forward_at(jnp.int32(total_steps - 1), incoming, saved)
    back_qkv, back_out = (
        lax.all_gather(w_qkv[0], "dp", axis=0, tiled=True),
        lax.all_gather(w_out[0], "dp", axis=1, tiled=True),
    )

    def backward_at(step, incoming, sum_qkv, sum_out):
        index = step - (sections - 1 - section)
        live = (index >= 0) & (index < micro)
        slot = jnp.clip(index, 0, micro - 1)
        last = lax.dynamic_index_in_dim(cotangent, slot, 0, keepdims=False)
        grad_y = jnp.where(section == sections - 1, last, incoming)
        x = lax.dynamic_index_in_dim(saved, slot, 0, keepdims=False)
        seg = lax.dynamic_index_in_dim(segs, slot, 0, keepdims=False)
        _, pull = jax.vjp(lambda a, b, c: layer(a, gain, b, c, seg), x, back_qkv, back_out)
        grad_x, grad_q, grad_o = pull(grad_y)
        sum_qkv = sum_qkv + jnp.where(live, grad_q.astype(jnp.float32), 0.0)
        sum_out = sum_out + jnp.where(live, grad_o.astype(jnp.float32), 0.0)
        return (grad_x, sum_qkv, sum_out)

    def backward_step(carry, step):
        incoming, sum_qkv, sum_out = carry
        grad_x, sum_qkv, sum_out = backward_at(step, incoming, sum_qkv, sum_out)
        incoming = passed_along(grad_x, "section", -1)
        return ((incoming, sum_qkv, sum_out), None)

    zero_qkv = jnp.zeros(back_qkv.shape, jnp.float32)
    zero_out = jnp.zeros(back_out.shape, jnp.float32)
    (incoming, sum_qkv, sum_out), _ = lax.scan(
        backward_step, (empty, zero_qkv, zero_out), jnp.arange(total_steps - 1, dtype=jnp.int32)
    )
    _, sum_qkv, sum_out = backward_at(jnp.int32(total_steps - 1), incoming, sum_qkv, sum_out)
    share_qkv, share_out = (
        lax.psum_scatter(sum_qkv, "dp", scatter_dimension=0, tiled=True),
        lax.psum_scatter(sum_out, "dp", scatter_dimension=1, tiled=True),
    )
    return (share_qkv[None], share_out[None])


def solution(mesh):
    return jax.shard_map(
        body,
        mesh=mesh,
        in_specs=(
            P(None, "dp", None),
            P(None, "dp", None),
            P(None, "dp", None),
            P("section", None),
            P("section", "dp", None),
            P("section", None, "dp"),
        ),
        out_specs=(P("section", "dp", None), P("section", None, "dp")),
        check_vma=False,
    )
```

profile of v0, /device:TPU:16, one launch (start us, length us, event | category | flops | bytes accessed | tf_op | source)
XLA Modules:
  0.0 1309.9 jit_solution(11713632534645186579)
XLA Ops:
  9.7 185.1 %all-gather.1 = bf16[1,64,4096]{1,0,2:T(2,128)(2,1)S(1)} all-gather(bf16[1,64,64]{1,0,2:T(2,128)(2,1)S(1)} %copy.16), channel_id=3, replica_groups=mesh['section'=8,'dp'=64] {'dp'}, dimensions={2}, use_global_device_ids=true | all-gather | bytes 532480 | tf_op jit(solution)/shard_map/all_gather | solution.py:48
  194.7 3.6 copy.17
  198.5 120.8 %all-gather.4.cloned.1.call-done = bf16[1,4096,192]{2,1,0:T(8,128)(2,1)} async-done(((bf16[1,64,192]{2,1,0:T(8,128)(2,1)}), bf16[1,4096,192]{2,1,0:T(8,128)(2,1)}) %all-gather.4.cloned.1.call-update) | async-done | bytes 1572880 | tf_op jit(solution)/shard_map/all_gather | solution.py:47
  320.3 157.4 %while.30 = (s32[]{:T(128)}, bf16[64,4096]{1,0:T(8,128)(2,1)}, bf16[2,64,4096]{2,1,0:T(8,128)(2,1)S(1)}, pred[]{:T(512)}, s32[8]{0:T(128)S(1)}, /*index=5*/s32[]...) while((s32[]{:T(128)}, bf16[64,4096]{1,0:T(8,128)(2,1)}, ...), condition=%wide.region_6.7_spmd, body=%wide.region_2.6_spmd.sunk | while | flops 138477504 | bytes 20632148 | solution.py:72
  326.7 1.9 collective-permute-start
  328.6 9.6 collective-permute-done
  345.4 1.9 collective-permute-start
  347.3 9.6 collective-permute-done
  364.1 12.1 collective-permute-start
  384.8 11.2 collective-permute-start
  404.7 11.1 collective-permute-start
  424.6 11.1 collective-permute-start
  444.4 11.1 collective-permute-start
  464.2 11.2 collective-permute-start
  481.1 157.0 %while.31 = (s32[]{:T(128)}, bf16[64,4096]{1,0:T(8,128)(2,1)}, f32[4096,192]{0,1:T(8,128)}, f32[64,4096]{1,0:T(8,128)}, pred[]{:T(512)}, /*index=5*/s32[8]{0:T(1...) while((s32[]{:T(128)}, bf16[64,4096]{1,0:T(8,128)(2,1)}, ...), condition=%wide.region_13.14_spmd.clone, body=%wide.region_7.13_spmd.clone.sunk | while | flops 384602496 | bytes 32000636 | solution.py:103
  487.8 1.9 collective-permute-start.1
  489.7 2.6 fusion.168
  492.2 2.4 fusion.167
  494.6 6.0 collective-permute-done.1
  507.3 1.9 collective-permute-start.1
  509.2 2.9 fusion.168
  512.1 4.3 fusion.167
  516.4 4.6 collective-permute-done.1
  527.6 1.9 collective-permute-start.1
  529.5 2.9 fusion.168
  532.4 4.3 fusion.167
  536.6 3.8 collective-permute-done.1
  549.0 2.9 fusion.168
  551.9 4.3 fusion.167
  556.2 3.8 collective-permute-done.1
  568.5 2.9 fusion.168
  571.4 4.3 fusion.167
  575.7 3.8 collective-permute-done.1
  588.1 2.9 fusion.168
  591.0 4.3 fusion.167
  595.2 3.8 collective-permute-done.1
  607.6 2.9 fusion.168
  610.5 4.3 fusion.167
  614.8 3.8 collective-permute-done.1
  627.1 2.9 fusion.168
  630.0 4.3 fusion.167
  634.3 3.8 collective-permute-done.1
  638.1 2.1 fusion.56
  640.2 2.0 copy.19
  642.3 5.2 copy.18
  649.6 5.0 fusion.53
  654.6 323.6 %reduce-scatter.7.cloned.1.call-done = f32[64,64]{1,0:T(8,128)} async-done(((f32[4096,64]{1,0:T(8,128)}), f32[64,64]{1,0:T(8,128)}) %reduce-scatter.7.cloned.1.call-update) | async-done | bytes 16400
  979.7 323.7 %reduce-scatter.5.cloned.1.call-done = f32[64,192]{1,0:T(8,128)} async-done(((f32[4096,192]{1,0:T(8,128)}), f32[64,192]{1,0:T(8,128)}) %reduce-scatter.5.cloned.1.call-update) | async-done | bytes 49168 | tf_op jit(solution)/shard_map/reduce_scatter | solution.py:108
  (398 shorter events, 128.2 us)
Async XLA Ops:
  7.2 191.2 %copy-start.9 = (bf16[1,4096]{1,0:T(2,128)(2,1)S(1)}, bf16[1,4096]{1,0:T(2,128)(2,1)}, u32[]{:S(2)}) copy-start(bf16[1,4096]{1,0:T(2,128)(2,1)} %param.13) | copy-start | bytes 24580
  7.2 312.2 %all-gather.4.cloned.1.call-start = ((), (), s32[]{:S(2)}) async-start(), calls=%async_computation.3 | async-start | bytes 2129920 | tf_op jit(solution)/shard_map/all_gather | solution.py:47
  7.9 970.3 %reduce-scatter.7.cloned.1.call-start = ((), (), s32[]{:S(2)}) async-start(), calls=%async_computation.4 | async-start | bytes 2129920
  320.3 3.9 copy-start
  326.7 11.5 collective-permute-start
  339.0 3.9 copy-start
  345.4 11.5 collective-permute-start
  357.6 3.9 copy-start
  364.1 13.6 %collective-permute-start = (bf16[64,4096]{1,0:T(8,128)(2,1)S(1)}, bf16[64,4096]{1,0:T(8,128)(2,1)S(1)}, u32[]{:S(2)}, u32[]{:S(2)}) collective-permute-start(bf16[64,4096]{1,0:T(8,128)(2,1)S(1)} %fusion.145), channel_id=1, source_target_pairs={{0,64},{64,128},{128,192},{192,256},{256,320},{320,384},{384,448},... | collective-permute-start | bytes 1572872 | tf_op jit(solution)/shard_map/while/body/eval_jaxpr/ppermute | solution.py:10
  378.4 3.9 copy-start
  384.8 12.7 collective-permute-start
  398.3 3.9 copy-start
  404.7 12.7 collective-permute-start
  418.2 3.9 copy-start
  424.6 12.6 collective-permute-start
  438.0 3.9 copy-start
  444.4 12.6 collective-permute-start
  457.8 3.9 copy-start
  464.2 12.7 collective-permute-start
  477.6 1.9 copy-start.1
  482.4 1.2 copy-start.7
  482.4 2.3 copy-start.4
  484.7 3.0 copy-start.2
  487.8 12.9 collective-permute-start.1
  501.9 2.3 copy-start.4
  504.2 3.0 copy-start.2
  507.3 13.7 %collective-permute-start.1 = (bf16[64,4096]{1,0:T(8,128)(2,1)}, bf16[64,4096]{1,0:T(8,128)(2,1)}, u32[]{:S(2)}, u32[]{:S(2)}) collective-permute-start(bf16[64,4096]{1,0:T(8,128)(2,1)} %fusion.166), channel_id=1, source_target_pairs={{64,0},{128,64},{192,128},{256,192},{320,256},{384,320},{448,384},... | collective-permute-start | bytes 1572872 | tf_op jit(solution)/shard_map/while/body/eval_jaxpr/ppermute | solution.py:10
  522.2 2.3 copy-start.4
  524.5 3.0 copy-start.2
  527.6 12.9 collective-permute-start.1
  541.7 2.3 copy-start.4
  544.0 3.0 copy-start.2
  547.1 12.9 collective-permute-start.1
  561.3 2.3 copy-start.4
  563.6 3.0 copy-start.2
  566.6 12.9 collective-permute-start.1
  580.8 2.3 copy-start.4
  583.1 3.0 copy-start.2
  586.1 12.9 collective-permute-start.1
  600.3 2.3 copy-start.4
  602.6 3.0 copy-start.2
  605.7 12.9 collective-permute-start.1
  619.8 2.3 copy-start.4
  622.2 3.0 copy-start.2
  625.2 12.9 collective-permute-start.1
  642.2 661.2 %reduce-scatter.5.cloned.1.call-start = ((), (), s32[]{:S(2)}) async-start(), calls=%async_computation.2 | async-start | bytes 4259840 | tf_op jit(solution)/shard_map/reduce_scatter | solution.py:108
  642.2 5.3 copy-start.5
  642.3 5.3 copy-start.8
  (23 other events, 21.2 us)
Sparse Core Ops, SparseCore 0:
  10.1 309.1 all-gather.3
  642.3 335.8 reduce-scatter.6
  981.8 321.5 reduce-scatter.4
where the time goes:
time: 1310 us
  waiting for transfers between devices  831 us (63%)
  blocking collectives  185 us (14%)
  matrix products  104 us (8%)
  starting transfers between devices  87 us (7%)
  local copies, waits for them, and re-layouts  39.2 us (3%)
  other arithmetic  38.6 us (3%)
  between operations  13.9 us (1%)
    unnamed x4, waiting for transfers between devices  324 us
    reduce_scatter x1, waiting for transfers between devices, body(): lax.psum_scatter(sum_qkv, 'dp', scatter_dimension=0, tiled=True)  324 us
    all_gather x1, blocking collectives, body(): lax.all_gather(w_out[0], 'dp', axis=1, tiled=True)  185 us
    all_gather x1, waiting for transfers between devices, body(): lax.all_gather(w_qkv[0], 'dp', axis=0, tiled=True)  121 us
    ppermute x16, starting transfers between devices, passed_along(): return lax.ppermute(block, axis, route)  86.9 us
    ppermute x16, waiting for transfers between devices, passed_along(): return lax.ppermute(block, axis, route)  61.8 us
    dot_general x34, matrix products, layer(): jnp.dot(normed, w_qkv, preferred_element_type=jnp.float32)  52.9 us
    dot_general x26, matrix products, layer(): jnp.dot(attended, w_out, preferred_element_type=jnp.float32)  41.8 us
  transfers between devices with their start and end apart: 19, of which 19 were waited for; matrix products, arithmetic and copies ran while one was open for 6% of the time, Pallas kernels for 0%

commit v1 on v0

--- a/solution.py
+++ b/solution.py
@@ -45,7 +45,9 @@
     gain = norm_gain[0]
     full_qkv, full_out = (
         lax.all_gather(w_qkv[0], "dp", axis=0, tiled=True),
-        lax.all_gather(w_out[0], "dp", axis=1, tiled=True),
+        jnp.concatenate(
+            lax.all_to_all(jnp.stack([w_out[0]] * lax.axis_size("dp")), "dp", 0, 0), axis=1
+        ),
     )
     total_steps = micro + sections - 1
     empty = jnp.zeros(inputs.shape[1:], inputs.dtype)

time: 1310 us -> 1310 us (level)
  waiting for transfers between devices: 831 us -> 814 us
  starting transfers between devices: 87 us -> 102 us
    all_to_all x0 -> x1, starting transfers between devices: none -> 14.9 us  [body(): lax.all_to_all(jnp.stack([w_out[0]] * lax.axis_size('dp')), 'dp', 0, 0)]
  transfers between devices with their start and end apart: 19 -> 20, of which waited for: 19 -> 19; matrix products, arithmetic and copies ran while one was open for 6% -> 6% of each run, Pallas kernels for 0% -> 0%
where the time goes in v1:
time: 1310 us
  waiting for transfers between devices  814 us (62%)
  blocking collectives  179 us (14%)
  matrix products  104 us (8%)
  starting transfers between devices  102 us (8%)
  local copies, waits for them, and re-layouts  44.2 us (3%)
  other arithmetic  38 us (3%)
  between operations  14 us (1%)
    reduce_scatter x1, waiting for transfers between devices, body(): lax.psum_scatter(sum_qkv, 'dp', scatter_dimension=0, tiled=True)  323 us
    unnamed x4, waiting for transfers between devices  321 us
    all_gather x1, blocking collectives, body(): lax.all_gather(w_out[0], 'dp', axis=1, tiled=True)  179 us
    all_gather x1, waiting for transfers between devices, body(): lax.all_gather(w_qkv[0], 'dp', axis=0, tiled=True)  108 us
    ppermute x16, starting transfers between devices, passed_along(): return lax.ppermute(block, axis, route)  86.6 us
    ppermute x16, waiting for transfers between devices, passed_along(): return lax.ppermute(block, axis, route)  61.8 us
    dot_general x34, matrix products, layer(): jnp.dot(normed, w_qkv, preferred_element_type=jnp.float32)  52.9 us
    dot_general x26, matrix products, layer(): jnp.dot(attended, w_out, preferred_element_type=jnp.float32)  41.8 us
  transfers between devices with their start and end apart: 20, of which 19 were waited for; matrix products, arithmetic and copies ran while one was open for 6% of the time, Pallas kernels for 0%

profile of v1, /device:TPU:16, one launch (start us, length us, event | category | flops | bytes accessed | tf_op | source)
XLA Modules:
  0.0 1306.6 jit_solution(3197488363103180503)
XLA Ops:
  10.4 14.9 %all-to-all-start = ((bf16[64,2,2048]{2,1,0:T(2,128)(2,1)}), bf16[64,2,2048]{2,1,0:T(2,128)(2,1)S(1)}, u32[]{:S(2)}, u32[]{:S(2)}) async-start(bf16[64,2,2048]{2,1,0:T(2,128)(2,1)} %reshape.103), calls=%async_computation | async-start | bytes 1048576 | tf_op jit(solution)/shard_map/all_to_all | solution.py:49
  25.8 179.0 %all-gather.1 = bf16[1,64,4096]{1,0,2:T(2,128)(2,1)S(1)} all-gather(bf16[1,64,64]{1,0,2:T(2,128)(2,1)S(1)} %copy.17), channel_id=3, replica_groups=mesh['section'=8,'dp'=64] {'dp'}, dimensions={2}, use_global_device_ids=true | all-gather | bytes 532480 | tf_op jit(solution)/shard_map/all_gather | solution.py:80
  204.7 3.6 copy.18
  211.5 108.2 %all-gather.4.cloned.1.call-done = bf16[1,4096,192]{2,1,0:T(8,128)(2,1)} async-done(((bf16[1,64,192]{2,1,0:T(8,128)(2,1)}), bf16[1,4096,192]{2,1,0:T(8,128)(2,1)}) %all-gather.4.cloned.1.call-update) | async-done | bytes 1572880 | tf_op jit(solution)/shard_map/all_gather | solution.py:47
  320.7 157.3 %while.30 = (s32[]{:T(128)}, bf16[64,4096]{1,0:T(8,128)(2,1)}, bf16[2,64,4096]{2,1,0:T(8,128)(2,1)S(1)}, pred[]{:T(512)}, s32[8]{0:T(128)S(1)}, /*index=5*/s32[]...) while((s32[]{:T(128)}, bf16[64,4096]{1,0:T(8,128)(2,1)}, ...), condition=%wide.region_6.7_spmd, body=%wide.region_2.6_spmd.sunk | while | flops 138477504 | bytes 20632148 | solution.py:74
  327.1 1.9 collective-permute-start
  329.1 9.6 collective-permute-done
  345.8 1.9 collective-permute-start
  347.8 9.6 collective-permute-done
  364.5 11.8 collective-permute-start
  385.1 11.2 collective-permute-start
  405.0 11.1 collective-permute-start
  424.9 11.1 collective-permute-start
  444.7 11.1 collective-permute-start
  464.5 11.1 collective-permute-start
  481.5 157.0 %while.31 = (s32[]{:T(128)}, bf16[64,4096]{1,0:T(8,128)(2,1)}, f32[4096,192]{0,1:T(8,128)}, f32[64,4096]{1,0:T(8,128)}, pred[]{:T(512)}, /*index=5*/s32[8]{0:T(1...) while((s32[]{:T(128)}, bf16[64,4096]{1,0:T(8,128)(2,1)}, ...), condition=%wide.region_13.14_spmd.clone, body=%wide.region_7.13_spmd.clone.sunk | while | flops 384602496 | bytes 32000636 | solution.py:105
  488.1 1.9 collective-permute-start.1
  490.0 2.6 fusion.168
  492.6 2.4 fusion.167
  495.0 6.0 collective-permute-done.1
  507.6 1.9 collective-permute-start.1
  509.5 2.9 fusion.168
  512.4 4.3 fusion.167
  516.7 4.6 collective-permute-done.1
  529.8 2.9 fusion.168
  532.7 4.3 fusion.167
  537.0 3.8 collective-permute-done.1
  549.3 2.9 fusion.168
  552.2 4.3 fusion.167
  556.5 3.8 collective-permute-done.1
  568.9 2.9 fusion.168
  571.8 4.3 fusion.167
  576.0 3.8 collective-permute-done.1
  588.4 2.9 fusion.168
  591.3 4.3 fusion.167
  595.6 3.8 collective-permute-done.1
  607.9 2.9 fusion.168
  610.8 4.3 fusion.167
  615.1 3.8 collective-permute-done.1
  627.5 2.9 fusion.168
  630.4 4.3 fusion.167
  634.6 3.8 collective-permute-done.1
  638.4 2.1 fusion.56
  640.5 2.0 copy.20
  642.6 5.2 copy.19
  649.9 5.0 fusion.53
  654.9 320.3 %reduce-scatter.7.cloned.1.call-done = f32[64,64]{1,0:T(8,128)} async-done(((f32[4096,64]{1,0:T(8,128)}), f32[64,64]{1,0:T(8,128)}) %reduce-scatter.7.cloned.1.call-update) | async-done | bytes 16400
  976.6 323.4 %reduce-scatter.5.cloned.1.call-done = f32[64,192]{1,0:T(8,128)} async-done(((f32[4096,192]{1,0:T(8,128)}), f32[64,192]{1,0:T(8,128)}) %reduce-scatter.5.cloned.1.call-update) | async-done | bytes 49168 | tf_op jit(solution)/shard_map/reduce_scatter | solution.py:110
  (409 shorter events, 134.4 us)
Async XLA Ops:
  7.2 18.3 %copy-start.9 = (bf16[1,64,64]{2,1,0:T(8,128)(2,1)S(1)}, bf16[1,64,64]{2,1,0:T(8,128)(2,1)}, u32[]{:S(2)}) copy-start(bf16[1,64,64]{2,1,0:T(8,128)(2,1)} %param.15) | copy-start | bytes 24580
  7.2 18.4 %copy-start.11 = (s32[2,1,2]{2,1,0:T(1,128)S(1)}, s32[2,1,2]{2,1,0:T(1,128)}, u32[]{:S(2)}) copy-start(s32[2,1,2]{2,1,0:T(1,128)} %param.12) | copy-start | bytes 52
  7.2 312.6 %all-gather.4.cloned.1.call-start = ((), (), s32[]{:S(2)}) async-start(), calls=%async_computation.4 | async-start | bytes 2129920 | tf_op jit(solution)/shard_map/all_gather | solution.py:47
  10.4 197.9 %copy-start.10 = (bf16[1,4096]{1,0:T(2,128)(2,1)S(1)}, bf16[1,4096]{1,0:T(2,128)(2,1)}, u32[]{:S(2)}) copy-start(bf16[1,4096]{1,0:T(2,128)(2,1)} %param.13) | copy-start | bytes 24580
  10.4 198.1 %all-to-all-start = ((bf16[64,2,2048]{2,1,0:T(2,128)(2,1)}), bf16[64,2,2048]{2,1,0:T(2,128)(2,1)S(1)}, u32[]{:S(2)}, u32[]{:S(2)}) async-start(bf16[64,2,2048]{2,1,0:T(2,128)(2,1)} %reshape.103), calls=%async_computation | async-start | bytes 1048576 | tf_op jit(solution)/shard_map/all_to_all | solution.py:49
  25.4 949.8 %reduce-scatter.7.cloned.1.call-start = ((), (), s32[]{:S(2)}) async-start(), calls=%async_computation.5 | async-start | bytes 2129920
  320.7 3.9 copy-start
  327.1 11.5 collective-permute-start
  339.4 3.9 copy-start
  345.8 11.5 collective-permute-start
  358.1 3.9 copy-start
  364.5 13.3 %collective-permute-start = (bf16[64,4096]{1,0:T(8,128)(2,1)S(1)}, bf16[64,4096]{1,0:T(8,128)(2,1)S(1)}, u32[]{:S(2)}, u32[]{:S(2)}) collective-permute-start(bf16[64,4096]{1,0:T(8,128)(2,1)S(1)} %fusion.145), channel_id=1, source_target_pairs={{0,64},{64,128},{128,192},{192,256},{256,320},{320,384},{384,448},... | collective-permute-start | bytes 1572872 | tf_op jit(solution)/shard_map/while/body/eval_jaxpr/ppermute | solution.py:10
  378.7 3.9 copy-start
  385.1 12.7 collective-permute-start
  398.6 3.9 copy-start
  405.0 12.7 collective-permute-start
  418.5 3.9 copy-start
  424.9 12.6 collective-permute-start
  438.3 3.9 copy-start
  444.7 12.6 collective-permute-start
  458.1 3.9 copy-start
  464.5 12.7 collective-permute-start
  485.1 3.0 copy-start.2
  488.1 12.9 collective-permute-start.1
  502.3 2.3 copy-start.5
  504.6 3.0 copy-start.2
  507.6 13.7 %collective-permute-start.1 = (bf16[64,4096]{1,0:T(8,128)(2,1)}, bf16[64,4096]{1,0:T(8,128)(2,1)}, u32[]{:S(2)}, u32[]{:S(2)}) collective-permute-start(bf16[64,4096]{1,0:T(8,128)(2,1)} %fusion.166), channel_id=1, source_target_pairs={{64,0},{128,64},{192,128},{256,192},{320,256},{384,320},{448,384},... | collective-permute-start | bytes 1572872 | tf_op jit(solution)/shard_map/while/body/eval_jaxpr/ppermute | solution.py:10
  522.5 2.3 copy-start.5
  524.8 3.0 copy-start.2
  527.9 12.9 collective-permute-start.1
  542.1 2.3 copy-start.5
  544.4 3.0 copy-start.2
  547.4 12.9 collective-permute-start.1
  561.6 2.3 copy-start.5
  563.9 3.0 copy-start.2
  566.9 12.9 collective-permute-start.1
  581.1 2.3 copy-start.5
  583.4 3.0 copy-start.2
  586.5 12.9 collective-permute-start.1
  600.6 2.3 copy-start.5
  603.0 3.0 copy-start.2
  606.0 12.9 collective-permute-start.1
  620.2 2.3 copy-start.5
  622.5 3.0 copy-start.2
  625.5 12.9 collective-permute-start.1
  642.5 657.5 %reduce-scatter.5.cloned.1.call-start = ((), (), s32[]{:S(2)}) async-start(), calls=%async_computation.3 | async-start | bytes 4259840 | tf_op jit(solution)/shard_map/reduce_scatter | solution.py:110
  642.6 5.3 copy-start.6
  642.6 5.3 copy-start.8
  (26 other events, 27.1 us)
Sparse Core Ops, SparseCore 0:
  10.1 309.6 all-gather.3
  642.6 332.4 reduce-scatter.6
  978.8 321.2 reduce-scatter.4
